TPU v7x, 32 devices: a whole 2x2x4 slice. The times are simulated.
32 devices in a mesh: groups: 2 (over y), rows: 16 (over z, x, core).
Axes of the slice: x: 2, y: 2, z: 4, core: 2. Of those that a mesh axis runs over, the one named last changes fastest.
Arguments:
- images: bfloat16 [2, 256, 256, 256], P(None, ('groups', 'rows')), parts along dimension 1, may hold values from -6 to 6
- third_weight: bfloat16 [3, 3, 256, 256], replicated, may hold values from -0.125 to 0.125
- third_bias: float32 [256], replicated, may hold values from -3 to 3
- fourth_weight: bfloat16 [3, 3, 256, 512], replicated, may hold values from -0.125 to 0.125
- fourth_bias: float32 [512], replicated, may hold values from -3 to 3
- third_linear: float32 [256], replicated, may hold values from 8 to 64
- fourth_linear: float32 [512], replicated, may hold values from 8 to 64
Outputs:
- input_grad: float32 [256, 256, 256], P(('groups', 'rows')), parts along dimension 0
There are 2 independent parts, one for each index of `groups`. A program takes and returns all parts, laid end to end along the dimension named above; an argument that names none is the same for every part. Nothing has to cross between parts.
All inputs are finite; a program needn't handle non-finite values.
Results may differ from a plain program's by a relative error of at most 0.0085.
Values may be sent and summed in bfloat16 or wider, within the bound.
A program may use at most 128 MiB of HBM per device.

v0:
```python
import jax
import jax.numpy as jnp
from jax import lax
from jax.sharding import PartitionSpec as P

EPS = 1e-06


def padded_2(block, sides, width):
    for axis, dim in sides:
        count = lax.axis_size(axis)
        forward = [(i, i + 1) for i in range(count - 1)]
        backward = [(target, source) for source, target in forward]
        low = lax.ppermute(
            lax.slice_in_dim(block, block.shape[dim] - width, None, axis=dim), axis, forward
        )
        high = lax.ppermute(lax.slice_in_dim(block, 0, width, axis=dim), axis, backward)
        block = jnp.concatenate([low, block, high], axis=dim)
    return block


def conv_rows(padded, weight, bias):
    stacks, rows_in, width, chans = padded.shape
    height = rows_in - 2
    widened = jnp.pad(padded, ((0, 0), (0, 0), (1, 1), (0, 0)))
    total = jnp.zeros((stacks * height * width, weight.shape[3]), jnp.float32)
    for offset in range(3):
        strip = widened[:, offset : offset + height]
        joined = jnp.concatenate(
            [strip[:, :, 0:width], strip[:, :, 1 : width + 1], strip[:, :, 2 : width + 2]], axis=3
        )
        total = total + jnp.dot(
            joined.reshape(-1, 3 * chans),
            weight[offset].reshape(3 * chans, -1),
            preferred_element_type=jnp.float32,
        )
    return total.reshape(stacks, height, width, -1) + bias


def conv_back(padded, weight):
    height = padded.shape[0] - 2
    width = padded.shape[1]
    outputs = weight.shape[3]
    widened = jnp.pad(padded, ((0, 0), (1, 1), (0, 0)))
    total = jnp.zeros((height * width, weight.shape[2]), jnp.float32)
    for offset in range(3):
        strip = widened[2 - offset : 2 - offset + height]
        joined = jnp.concatenate(
            [strip[:, 2 - step : 2 - step + width] for step in range(3)], axis=2
        )
        flipped = jnp.transpose(weight[offset], (0, 2, 1)).reshape(3 * outputs, -1)
        total = total + jnp.dot(
            joined.reshape(-1, 3 * outputs), flipped, preferred_element_type=jnp.float32
        )
    return total.reshape(height, width, -1)


def silu_grad(pre):
    sig = jax.nn.sigmoid(pre)
    return sig * (1.0 + pre * (1.0 - sig))


def lpips_grad(first, second, linear):
    chans = first.shape[-1]
    scale_first = jnp.sqrt(jnp.sum(first * first, -1, keepdims=True) + chans * EPS)
    scale_second = jnp.sqrt(jnp.sum(second * second, -1, keepdims=True) + chans * EPS)
    unit_first = first / scale_first
    weighted = linear * (unit_first - second / scale_second)
    return (
        2.0
        * (weighted - unit_first * jnp.sum(weighted * unit_first, -1, keepdims=True))
        / scale_first
    )


def pool_mean(field):
    stacks, height, width, chans = field.shape
    blocks = field.astype(jnp.float32).reshape(stacks, height // 2, 2, width // 2, 2, chans)
    return jnp.mean(blocks, axis=(2, 4))


def upsample(field):
    height, width, chans = field.shape
    grown = jnp.broadcast_to(field[:, None, :, None, :], (height, 2, width, 2, chans))
    return 0.25 * grown.reshape(2 * height, 2 * width, chans)


def mask_rows(field, first_row, limit, axis_pos):
    count = field.shape[axis_pos]
    global_rows = first_row + lax.iota(jnp.int32, count)
    keep = (global_rows >= 0) & (global_rows < limit)
    shape = [1] * field.ndim
    shape[axis_pos] = count
    return jnp.where(keep.reshape(shape), field, jnp.zeros((), field.dtype))


def local(
    images, third_weight, third_bias, fourth_weight, fourth_bias, third_linear, fourth_linear
):
    tile_rows = images.shape[1]
    half_rows = tile_rows // 2
    position = lax.axis_index("rows")
    band_rows = tile_rows * lax.axis_size("rows")
    wide_images = padded_2(images, (("rows", 1),), 1)
    pre3 = conv_rows(wide_images, third_weight, third_bias)
    reach3 = (pre3.shape[1] - tile_rows) // 2
    act3 = jax.nn.silu(pre3).astype(jnp.bfloat16)
    pooled = pool_mean(act3)
    reach_pool = reach3 // 2
    pooled = mask_rows(pooled, position * half_rows - reach_pool, band_rows // 2, 1).astype(
        jnp.bfloat16
    )
    wide_pooled = padded_2(pooled, (("rows", 1),), 1)
    pre4 = conv_rows(wide_pooled, fourth_weight, fourth_bias)
    reach4 = (pre4.shape[1] - half_rows) // 2
    act4 = jax.nn.silu(pre4)
    grad4 = lpips_grad(act4[0], act4[1], fourth_linear) * silu_grad(pre4[0])
    grad4 = mask_rows(grad4, position * half_rows - reach4, band_rows // 2, 0).astype(jnp.bfloat16)
    wide_grad4 = padded_2(grad4, (("rows", 0),), 1)
    back4 = conv_back(wide_grad4, fourth_weight)
    reach_up = back4.shape[0] - half_rows
    cut = reach3 - reach_up
    act_mid = act3.astype(jnp.float32)
    pre_mid = pre3[0, cut : pre3.shape[1] - cut]
    grad3 = (upsample(back4) + lpips_grad(act_mid[0], act_mid[1], third_linear)) * silu_grad(
        pre_mid
    )
    grad3 = mask_rows(grad3, position * tile_rows - reach_up, band_rows, 0).astype(jnp.bfloat16)
    wide_grad3 = padded_2(grad3, (("rows", 0),), 1)
    return conv_back(wide_grad3, third_weight)


def solution(mesh):
    return jax.shard_map(
        local,
        mesh=mesh,
        in_specs=(P(None, ("groups", "rows"), None, None), P(), P(), P(), P(), P(), P()),
        out_specs=P(("groups", "rows"), None, None),
        check_vma=False,
    )
```

profile of v0, /device:TPU:1, one launch (start us, length us, event | category | flops | bytes accessed | tf_op | source)
XLA Modules:
  0.0 119.6 jit_solution(12945292601875421503)
XLA Ops:
  0.0 1.9 %fusion.69 = (bf16[2,1,256,256]{3,2,1,0:T(8,128)(2,1)}, bf16[2,1,256,256]{3,2,1,0:T(8,128)(2,1)}) fusion(bf16[2,8,256,256]{3,2,1,0:T(8,128)(2,1)} %param.7), kind=kLoop, calls=%fused_computation.122 | loop fusion | bytes 1048576 | tf_op jit(solution)/shard_map/slice | solution.py:15
  1.9 4.5 %collective-permute-start = (bf16[2,1,256,256]{3,2,1,0:T(8,128)(2,1)}, bf16[2,1,256,256]{3,2,1,0:T(8,128)(2,1)S(1)}, u32[]{:S(2)}, u32[]{:S(2)}) collective-permute-start(bf16[2,1,256,256]{3,2,1,0:T(8,128)(2,1)} %get-tuple-element.28), channel_id=1, source_target_pairs={{0,1},{1,2},{2,3},{3,4},{4,5},{5,6},{6,7},{7,8},{8,9},{9,10},{10,1... | collective-permute-start | bytes 786440 | tf_op jit(solution)/shard_map/ppermute | solution.py:14
  6.4 1.9 %collective-permute-start.1 = (bf16[2,1,256,256]{3,2,1,0:T(8,128)(2,1)}, bf16[2,1,256,256]{3,2,1,0:T(8,128)(2,1)}, u32[]{:S(2)}, u32[]{:S(2)}) collective-permute-start(bf16[2,1,256,256]{3,2,1,0:T(8,128)(2,1)} %get-tuple-element.29), channel_id=1, source_target_pairs={{1,0},{2,1},{3,2},{4,3},{5,4},{6,5},{7,6},{8,7},{9,8},{10,9},{11,1... | collective-permute-start | bytes 786440 | tf_op jit(solution)/shard_map/ppermute | solution.py:17
  8.3 3.2 %slice_bitcast_fusion.11 = (bf16[3,512,256]{1,2,0:T(8,128)(2,1)}, bf16[3,512,256]{1,2,0:T(8,128)(2,1)S(1)}, bf16[3,512,256]{1,2,0:T(8,128)(2,1)S(1)}, bf16[1,3,2...) fusion(bf16[3,3,256,512]{3,2,1,0:T(8,128)(2,1)} %param.10), kind=kLoop, calls=%fused_computation.120 | loop fusion | bytes 7077888 | tf_op jit(solution)/shard_map/transpose | solution.py:51
  11.5 1.2 copy.28
  12.7 1.2 copy.29
  13.9 2.4 %copy.27 = bf16[3,512,256]{2,1,0:T(8,128)(2,1)} copy(bf16[3,512,256]{1,2,0:T(8,128)(2,1)} %get-tuple-element.19) | data formatting | bytes 1572864 | tf_op jit(solution)/shard_map/transpose | solution.py:51
  16.3 2.4 %slice_bitcast_fusion.8 = (bf16[3,256,256]{1,2,0:T(8,128)(2,1)S(1)}, bf16[3,256,256]{1,2,0:T(8,128)(2,1)}, bf16[3,256,256]{1,2,0:T(8,128)(2,1)}, bf16[1,3,256,25...) fusion(bf16[3,3,256,256]{3,2,1,0:T(8,128)(2,1)} %param.8), kind=kLoop, calls=%fused_computation.117 | loop fusion | bytes 3538944 | tf_op jit(solution)/shard_map/transpose | solution.py:51
  18.7 0.0 collective-permute-done
  18.7 1.8 %fusion.16 = bf16[2,10,258,256]{3,2,1,0:T(8,128)(2,1)S(1)} fusion(bf16[2,1,256,256]{3,2,1,0:T(8,128)(2,1)} %collective-permute-done.1, bf16[2,8,256,256]{3,2,1,0:T(8,128)(2,1)S(1)} %copy-done.2, bf16[2,1,256,256]{3,2,1,0:T(8,128)(2,1)S(1)} %collective-permute-done), kind=kLoop, calls=%fused_computation.32 | loop fusion | flops 15851520 | bytes 5263360 | tf_op jit(solution)/shard_map/concatenate | solution.py:18
  20.5 4.4 %fusion.68 = (bf16[2,8,256,256]{3,2,1,0:T(8,128)(2,1)S(1)}, bf16[2,8,256,256]{3,2,1,0:T(8,128)(2,1)}, bf16[2,8,256,256]{3,2,1,0:T(8,128)(2,1)}, bf16[2,8,256,256...) fusion(bf16[2,10,258,256]{3,2,1,0:T(8,128)(2,1)S(1)} %fusion.16), kind=kLoop, calls=%fused_computation.121 | loop fusion | bytes 25165824 | tf_op jit(solution)/shard_map/slice | solution.py:30
  24.8 6.3 %fusion.5 = (bf16[2,8,256,768]{3,2,1,0:T(8,128)(2,1)S(1)}, bf16[2,8,256,768]{3,2,1,0:T(8,128)(2,1)S(1)}, bf16[2,8,256,768]{3,2,1,0:T(8,128)(2,1)S(1)}) fusion(bf16[2,8,256,256]{3,2,1,0:T(8,128)(2,1)S(1)} %copy-done.2, bf16[2,1,256,256]{3,2,1,0:T(8,128)(2,1)S(1)} %collective-permute-done, bf16[2,8,256,256]{3,2,1,0:T(8,128)(2,1)} %get-tuple-element.17, ...), kind=kLoop, calls=%fused_computation.9 | loop fusion | flops 69206016 | bytes 34078720 | tf_op jit(solution)/shard_map/concatenate | solution.py:29
  31.1 1.9 %fusion.76 = f32[4096,256]{1,0:T(8,128)S(1)} fusion(bf16[4096,768]{1,0:T(8,128)(2,1)S(1)} %bitcast.144, bf16[768,256]{1,0:T(8,128)(2,1)S(1)} %bitcast.166), kind=kOutput, calls=%fused_computation.129 | convolution fusion | flops 1610612736 | bytes 10878976 | tf_op jit(solution)/shard_map/dot_general | solution.py:32
  33.0 1.9 %fusion.77 = f32[4096,256]{1,0:T(8,128)S(1)} fusion(bf16[4096,768]{1,0:T(8,128)(2,1)S(1)} %bitcast.143, bf16[768,256]{1,0:T(8,128)(2,1)S(1)} %bitcast.165), kind=kOutput, calls=%fused_computation.130 | convolution fusion | flops 1610612736 | bytes 10878976 | tf_op jit(solution)/shard_map/dot_general | solution.py:32
  34.9 4.0 %fusion.7 = f32[4096,256]{1,0:T(8,128)} fusion(f32[4096,256]{1,0:T(8,128)S(1)} %fusion.77, f32[4096,256]{1,0:T(8,128)S(1)} %fusion.76, bf16[4096,768]{1,0:T(8,128)(2,1)S(1)} %bitcast.145, bf16[768,256]{1,0:T(8,128)(2,1)S(1)} %bitcast.161), kind=kOutput, calls=%fused_computation.13 | convolution fusion | flops 1612709888 | bytes 19267584 | tf_op jit(solution)/shard_map/dot_general | solution.py:32
  38.9 5.9 %reshape.130 = f32[2,4,2,128,2,256]{5,4,3,2,1,0:T(2,128)} reshape(f32[4096,256]{1,0:T(8,128)} %fusion.7) | data formatting | bytes 8388608 | tf_op jit(solution)/shard_map/reshape | solution.py:37
  44.8 5.6 %fusion.19 = (f32[2,8,256,256]{3,2,1,0:T(8,128)S(1)}, f32[2,8,256,256]{3,2,1,0:T(8,128)}) fusion(f32[2,8,256,256]{3,2,1,0:T(8,128)} %bitcast.142, f32[256]{0:T(256)S(1)} %copy-done.10), kind=kLoop, calls=%fused_computation.39 | loop fusion | flops 7340032 | bytes 12583936 | tf_op jit(solution)/shard_map/convert_element_type | solution.py:78
  50.4 1.3 %convert_reduce_fusion = f32[2,4,128,256]{3,2,1,0:T(8,128)S(1)} fusion(f32[256]{0:T(256)S(1)} %copy-done.10, f32[2,4,2,128,2,256]{5,4,3,2,1,0:T(2,128)S(1)} %copy-done.1), kind=kLoop, calls=%fused_computation.16 | loop fusion | flops 8126464 | bytes 5243904 | tf_op jit(solution)/shard_map/reduce_sum | solution.py:79
  51.7 0.3 select_convert_fusion.1
  52.0 3.6 %collective-permute-start.2 = (bf16[2,1,128,256]{3,2,1,0:T(8,128)(2,1)S(1)}, bf16[2,1,128,256]{3,2,1,0:T(8,128)(2,1)S(1)}, u32[]{:S(2)}, u32[]{:S(2)}) collective-permute-start(bf16[2,1,128,256]{3,2,1,0:T(8,128)(2,1)S(1)} %get-tuple-element.68), channel_id=1, source_target_pairs={{0,1},{1,2},{2,3},{3,4},{4,5},{5,6},{6,7},{7,8},{8,9},{9,10},{10,1... | collective-permute-start | bytes 393224 | tf_op jit(solution)/shard_map/ppermute | solution.py:14
  55.6 1.9 %collective-permute-start.3 = (bf16[2,1,128,256]{3,2,1,0:T(8,128)(2,1)S(1)}, bf16[2,1,128,256]{3,2,1,0:T(8,128)(2,1)S(1)}, u32[]{:S(2)}, u32[]{:S(2)}) collective-permute-start(bf16[2,1,128,256]{3,2,1,0:T(8,128)(2,1)S(1)} %get-tuple-element.67), channel_id=1, source_target_pairs={{1,0},{2,1},{3,2},{4,3},{5,4},{6,5},{7,6},{8,7},{9,8},{10,9},{11,1... | collective-permute-start | bytes 393224 | tf_op jit(solution)/shard_map/ppermute | solution.py:17
  57.6 0.6 multiply_reduce_fusion.1
  58.2 3.7 %collective-permute-done.3 = bf16[2,1,128,256]{3,2,1,0:T(8,128)(2,1)S(1)} collective-permute-done((bf16[2,1,128,256]{3,2,1,0:T(8,128)(2,1)S(1)}, bf16[2,1,128,256]{3,2,1,0:T(8,128)(2,1)S(1)}, u32[]{:S(2)}, u32[]{:S(2)}) %collective-permute-start.3) | collective-permute-done | bytes 131104 | tf_op jit(solution)/shard_map/ppermute | solution.py:17
  61.9 0.2 fusion.60
  62.1 0.4 fusion.73
  62.6 0.5 fusion.30
  63.1 0.6 copy-done.9
  63.7 1.0 fusion.78
  64.7 0.2 copy-done.8
  64.9 1.0 fusion.79
  65.8 0.0 copy-start.11
  65.8 1.0 add_add_fusion
  66.8 0.0 copy-start.12
  66.9 0.7 divide_multiply_fusion
  67.5 0.2 multiply_reduce_fusion.3
  67.8 2.8 %fusion.44 = bf16[4,128,512]{2,1,0:T(8,128)(2,1)S(1)} fusion(f32[2,4,128,512]{3,2,1,0:T(8,128)S(1)} %get-tuple-element.12, f32[4,128]{1,0:T(4,128)S(1)} %get-tuple-element.70, f32[512]{0:T(512)S(1)} %copy-done.12, pred[4]{0:T(512)(128)(4,1)S(1)} %compare_and_fusion, f32[2,4,128,512]{3,2,1,0:T(8,128)S(1)} %get-tuple-element.11, ...), kind=kOutput, calls=%fused_computation.81 | output fusion | flops 6030335 | bytes 5779968 | tf_op jit(solution)/shard_map/mul | solution.py:71
  70.6 1.9 %collective-permute-start.4 = (bf16[1,128,512]{2,1,0:T(8,128)(2,1)S(1)}, bf16[1,128,512]{2,1,0:T(8,128)(2,1)S(1)}, u32[]{:S(2)}, u32[]{:S(2)}) collective-permute-start(bf16[1,128,512]{2,1,0:T(8,128)(2,1)S(1)} %get-tuple-element.63), channel_id=1, source_target_pairs={{0,1},{1,2},{2,3},{3,4},{4,5},{5,6},{6,7},{7,8},{8,9},{9,10},{10,1... | collective-permute-start | bytes 393224 | tf_op jit(solution)/shard_map/ppermute | solution.py:14
  72.5 2.4 %collective-permute-start.5 = (bf16[1,128,512]{2,1,0:T(8,128)(2,1)S(1)}, bf16[1,128,512]{2,1,0:T(8,128)(2,1)S(1)}, u32[]{:S(2)}, u32[]{:S(2)}) collective-permute-start(bf16[1,128,512]{2,1,0:T(8,128)(2,1)S(1)} %get-tuple-element.62), channel_id=1, source_target_pairs={{1,0},{2,1},{3,2},{4,3},{5,4},{6,5},{7,6},{8,7},{9,8},{10,9},{11,1... | collective-permute-start | bytes 393224 | tf_op jit(solution)/shard_map/ppermute | solution.py:17
  75.0 5.6 %collective-permute-done.5 = bf16[1,128,512]{2,1,0:T(8,128)(2,1)S(1)} collective-permute-done((bf16[1,128,512]{2,1,0:T(8,128)(2,1)S(1)}, bf16[1,128,512]{2,1,0:T(8,128)(2,1)S(1)}, u32[]{:S(2)}, u32[]{:S(2)}) %collective-permute-start.5) | collective-permute-done | bytes 131104 | tf_op jit(solution)/shard_map/ppermute | solution.py:17
  80.5 0.2 fusion.62
  80.7 0.4 fusion.72
  81.1 0.5 fusion.28
  81.7 0.6 copy-done.4
  82.3 0.6 fusion.80
  82.8 0.0 copy-done.3
  82.9 0.6 fusion.81
  83.4 0.0 copy-done.5
  83.4 0.6 fusion.46
  84.0 0.5 broadcast_in_dim.56
  84.6 0.0 copy-start.13
  84.6 2.4 %mul.130 = f32[8,256,256]{2,1,0:T(8,128)} reshape(f32[4,2,128,2,256]{4,3,2,1,0:T(2,128)S(1)} %broadcast_in_dim.56) | data formatting | bytes 4194304 | tf_op jit(solution)/shard_map/mul | solution.py:85
  87.0 16.5 %select_convert_fusion = bf16[8,256,256]{2,1,0:T(8,128)(2,1)S(1)} fusion(f32[2,8,256,256]{3,2,1,0:T(8,128)} %get-tuple-element.10, f32[8,256,256]{2,1,0:T(8,128)} %mul.130, f32[8,256]{1,0:T(8,128)S(1)} %get-tuple-element.72, f32[256]{0:T(256)S(1)} %copy-done.13, pred[8]{0:T(512)(128)(4,1)S(1)} %compare_and_fusion.1, f32[2,8,256,256]{3,2,1,0:T(8,128)} %copy-done, ...), kind=kOutput, calls=%fused_computation.43 | output fusion | flops 12585215 | bytes 13666816 | tf_op jit(solution)/shard_map/mul | solution.py:71
  103.6 1.9 %collective-permute-start.6 = (bf16[1,256,256]{2,1,0:T(8,128)(2,1)S(1)}, bf16[1,256,256]{2,1,0:T(8,128)(2,1)S(1)}, u32[]{:S(2)}, u32[]{:S(2)}) collective-permute-start(bf16[1,256,256]{2,1,0:T(8,128)(2,1)S(1)} %get-tuple-element.46), channel_id=1, source_target_pairs={{0,1},{1,2},{2,3},{3,4},{4,5},{5,6},{6,7},{7,8},{8,9},{9,10},{10,1... | collective-permute-start | bytes 393224 | tf_op jit(solution)/shard_map/ppermute | solution.py:14
  105.5 2.6 %collective-permute-start.7 = (bf16[1,256,256]{2,1,0:T(8,128)(2,1)S(1)}, bf16[1,256,256]{2,1,0:T(8,128)(2,1)S(1)}, u32[]{:S(2)}, u32[]{:S(2)}) collective-permute-start(bf16[1,256,256]{2,1,0:T(8,128)(2,1)S(1)} %get-tuple-element.45), channel_id=1, source_target_pairs={{1,0},{2,1},{3,2},{4,3},{5,4},{6,5},{7,6},{8,7},{9,8},{10,9},{11,1... | collective-permute-start | bytes 393224 | tf_op jit(solution)/shard_map/ppermute | solution.py:17
  108.2 0.2 copy.31
  108.3 0.2 copy.32
  108.5 0.2 copy.30
  108.7 4.0 %collective-permute-done.7 = bf16[1,256,256]{2,1,0:T(8,128)(2,1)S(1)} collective-permute-done((bf16[1,256,256]{2,1,0:T(8,128)(2,1)S(1)}, bf16[1,256,256]{2,1,0:T(8,128)(2,1)S(1)}, u32[]{:S(2)}, u32[]{:S(2)}) %collective-permute-start.7) | collective-permute-done | bytes 131104 | tf_op jit(solution)/shard_map/ppermute | solution.py:17
  112.7 0.3 fusion.42
  113.0 0.8 fusion.70
  113.9 1.2 fusion.11
  115.1 1.0 fusion.82
  116.1 1.0 fusion.83
  117.1 2.5 %fusion.18 = f32[2048,256]{1,0:T(8,128)} fusion(f32[2048,256]{1,0:T(8,128)S(1)} %fusion.83, f32[2048,256]{1,0:T(8,128)S(1)} %fusion.82, bf16[2048,768]{1,0:T(8,128)(2,1)S(1)} %bitcast.146, bf16[768,256]{1,0:T(8,128)(2,1)S(1)} %bitcast.162), kind=kOutput, calls=%fused_computation.34 | convolution fusion | flops 806354944 | bytes 9830400 | tf_op jit(solution)/shard_map/dot_general | solution.py:52
  (31 shorter events, 0.1 us)
Async XLA Ops:
  1.9 16.8 %collective-permute-start = (bf16[2,1,256,256]{3,2,1,0:T(8,128)(2,1)}, bf16[2,1,256,256]{3,2,1,0:T(8,128)(2,1)S(1)}, u32[]{:S(2)}, u32[]{:S(2)}) collective-permute-start(bf16[2,1,256,256]{3,2,1,0:T(8,128)(2,1)} %get-tuple-element.28), channel_id=1, source_target_pairs={{0,1},{1,2},{2,3},{3,4},{4,5},{5,6},{6,7},{7,8},{8,9},{9,10},{10,1... | collective-permute-start | bytes 786440 | tf_op jit(solution)/shard_map/ppermute | solution.py:14
  6.4 12.3 %collective-permute-start.1 = (bf16[2,1,256,256]{3,2,1,0:T(8,128)(2,1)}, bf16[2,1,256,256]{3,2,1,0:T(8,128)(2,1)}, u32[]{:S(2)}, u32[]{:S(2)}) collective-permute-start(bf16[2,1,256,256]{3,2,1,0:T(8,128)(2,1)} %get-tuple-element.29), channel_id=1, source_target_pairs={{1,0},{2,1},{3,2},{4,3},{5,4},{6,5},{7,6},{8,7},{9,8},{10,9},{11,1... | collective-permute-start | bytes 786440 | tf_op jit(solution)/shard_map/ppermute | solution.py:17
  13.9 4.8 %copy-start.2 = (bf16[2,8,256,256]{3,2,1,0:T(8,128)(2,1)S(1)}, bf16[2,8,256,256]{3,2,1,0:T(8,128)(2,1)}, u32[]{:S(2)}) copy-start(bf16[2,8,256,256]{3,2,1,0:T(8,128)(2,1)} %param.7) | copy-start | bytes 6291460
  38.9 5.9 %copy-start.10 = (f32[256]{0:T(256)S(1)}, f32[256]{0:T(256)}, u32[]{:S(2)}) copy-start(f32[256]{0:T(256)} %param.9) | copy-start | bytes 3076
  44.8 5.6 %copy-start.1 = (f32[2,4,2,128,2,256]{5,4,3,2,1,0:T(2,128)S(1)}, f32[2,4,2,128,2,256]{5,4,3,2,1,0:T(2,128)}, u32[]{:S(2)}) copy-start(f32[2,4,2,128,2,256]{5,4,3,2,1,0:T(2,128)} %reshape.130) | copy-start | bytes 12582916
  50.4 7.2 %copy-start = (f32[2,8,256,256]{3,2,1,0:T(8,128)}, f32[2,8,256,256]{3,2,1,0:T(8,128)S(1)}, u32[]{:S(2)}) copy-start(f32[2,8,256,256]{3,2,1,0:T(8,128)S(1)} %get-tuple-element.9) | copy-start | bytes 12582916
  52.0 6.2 %collective-permute-start.2 = (bf16[2,1,128,256]{3,2,1,0:T(8,128)(2,1)S(1)}, bf16[2,1,128,256]{3,2,1,0:T(8,128)(2,1)S(1)}, u32[]{:S(2)}, u32[]{:S(2)}) collective-permute-start(bf16[2,1,128,256]{3,2,1,0:T(8,128)(2,1)S(1)} %get-tuple-element.68), channel_id=1, source_target_pairs={{0,1},{1,2},{2,3},{3,4},{4,5},{5,6},{6,7},{7,8},{8,9},{9,10},{10,1... | collective-permute-start | bytes 393224 | tf_op jit(solution)/shard_map/ppermute | solution.py:14
  55.6 6.3 %collective-permute-start.3 = (bf16[2,1,128,256]{3,2,1,0:T(8,128)(2,1)S(1)}, bf16[2,1,128,256]{3,2,1,0:T(8,128)(2,1)S(1)}, u32[]{:S(2)}, u32[]{:S(2)}) collective-permute-start(bf16[2,1,128,256]{3,2,1,0:T(8,128)(2,1)S(1)} %get-tuple-element.67), channel_id=1, source_target_pairs={{1,0},{2,1},{3,2},{4,3},{5,4},{6,5},{7,6},{8,7},{9,8},{10,9},{11,1... | collective-permute-start | bytes 393224 | tf_op jit(solution)/shard_map/ppermute | solution.py:17
  62.6 1.1 copy-start.9
  63.7 1.1 copy-start.8
  65.8 1.0 copy-start.11
  66.8 0.9 copy-start.12
  70.6 4.4 %collective-permute-start.4 = (bf16[1,128,512]{2,1,0:T(8,128)(2,1)S(1)}, bf16[1,128,512]{2,1,0:T(8,128)(2,1)S(1)}, u32[]{:S(2)}, u32[]{:S(2)}) collective-permute-start(bf16[1,128,512]{2,1,0:T(8,128)(2,1)S(1)} %get-tuple-element.63), channel_id=1, source_target_pairs={{0,1},{1,2},{2,3},{3,4},{4,5},{5,6},{6,7},{7,8},{8,9},{9,10},{10,1... | collective-permute-start | bytes 393224 | tf_op jit(solution)/shard_map/ppermute | solution.py:14
  72.5 8.0 %collective-permute-start.5 = (bf16[1,128,512]{2,1,0:T(8,128)(2,1)S(1)}, bf16[1,128,512]{2,1,0:T(8,128)(2,1)S(1)}, u32[]{:S(2)}, u32[]{:S(2)}) collective-permute-start(bf16[1,128,512]{2,1,0:T(8,128)(2,1)S(1)} %get-tuple-element.62), channel_id=1, source_target_pairs={{1,0},{2,1},{3,2},{4,3},{5,4},{6,5},{7,6},{8,7},{9,8},{10,9},{11,1... | collective-permute-start | bytes 393224 | tf_op jit(solution)/shard_map/ppermute | solution.py:17
  81.1 1.1 copy-start.4
  81.7 1.2 copy-start.3
  82.3 1.2 copy-start.5
  84.6 2.5 %copy-start.13 = (f32[256]{0:T(256)S(1)}, f32[256]{0:T(256)}, u32[]{:S(2)}) copy-start(f32[256]{0:T(256)} %param.12) | copy-start | bytes 3076
  87.0 21.1 %copy-start.7 = (bf16[3,256,256]{1,2,0:T(8,128)(2,1)S(1)}, bf16[3,256,256]{1,2,0:T(8,128)(2,1)}, u32[]{:S(2)}) copy-start(bf16[3,256,256]{1,2,0:T(8,128)(2,1)} %get-tuple-element.37) | copy-start | bytes 1179652
  87.0 21.3 %copy-start.6 = (bf16[3,256,256]{1,2,0:T(8,128)(2,1)S(1)}, bf16[3,256,256]{1,2,0:T(8,128)(2,1)}, u32[]{:S(2)}) copy-start(bf16[3,256,256]{1,2,0:T(8,128)(2,1)} %get-tuple-element.38) | copy-start | bytes 1179652
  103.6 5.1 %collective-permute-start.6 = (bf16[1,256,256]{2,1,0:T(8,128)(2,1)S(1)}, bf16[1,256,256]{2,1,0:T(8,128)(2,1)S(1)}, u32[]{:S(2)}, u32[]{:S(2)}) collective-permute-start(bf16[1,256,256]{2,1,0:T(8,128)(2,1)S(1)} %get-tuple-element.46), channel_id=1, source_target_pairs={{0,1},{1,2},{2,3},{3,4},{4,5},{5,6},{6,7},{7,8},{8,9},{9,10},{10,1... | collective-permute-start | bytes 393224 | tf_op jit(solution)/shard_map/ppermute | solution.py:14
  105.5 7.2 %collective-permute-start.7 = (bf16[1,256,256]{2,1,0:T(8,128)(2,1)S(1)}, bf16[1,256,256]{2,1,0:T(8,128)(2,1)S(1)}, u32[]{:S(2)}, u32[]{:S(2)}) collective-permute-start(bf16[1,256,256]{2,1,0:T(8,128)(2,1)S(1)} %get-tuple-element.45), channel_id=1, source_target_pairs={{1,0},{2,1},{3,2},{4,3},{5,4},{6,5},{7,6},{8,7},{9,8},{10,9},{11,1... | collective-permute-start | bytes 393224 | tf_op jit(solution)/shard_map/ppermute | solution.py:17
where the time goes:
time: 120 us
  other arithmetic  39 us (32%)
  local copies, waits for them, and re-layouts  29.1 us (24%)
  starting transfers between devices  20.9 us (17%)
  matrix products  16.9 us (14%)
  waiting for transfers between devices  13.3 us (11%)
    mul x2, other arithmetic, lpips_grad(): unit_first * jnp.sum(weighted * unit_first, -1, keepdims=True)  19.3 us
    ppermute x4, waiting for transfers between devices, padded_2(): lax.ppermute(lax.slice_in_dim(block, 0, width, axis=dim), axis, backward)  13.3 us
    ppermute x4, starting transfers between devices, padded_2(): lax.ppermute(lax.slice_in_dim(block, block.shape[dim] - width, None, axis...  12 us
    transpose x8, local copies, waits for them, and re-layouts, conv_back(): flipped = jnp.transpose(weight[offset], (0, 2, 1)).reshape(3 * outputs, -1)  10.8 us
    dot_general x6, matrix products, conv_rows(): jnp.dot(joined.reshape(-1, 3 * chans), weight[offset].reshape(3 * chans,...  10.7 us
    ppermute x4, starting transfers between devices, padded_2(): lax.ppermute(lax.slice_in_dim(block, 0, width, axis=dim), axis, backward)  8.88 us
    concatenate x2, other arithmetic, conv_rows(): jnp.concatenate([strip[:, :, 0:width], strip[:, :, 1:width + 1], strip[:,...  6.78 us
    dot_general x6, matrix products, conv_back(): jnp.dot(joined.reshape(-1, 3 * outputs), flipped, preferred_element_type=...  6.21 us
  transfers between devices with their start and end apart: 8, of which 3 were waited for; matrix products, arithmetic and copies ran while one was open for 10% of the time, Pallas kernels for 0%

commit v1 on v0

v1 whole, which is shorter than its diff:
```python
import functools
import jax
import jax.numpy as jnp
from jax import lax
from jax.experimental import pallas as pl
from jax.experimental.pallas import tpu as pltpu
from jax.sharding import PartitionSpec as P

EPS = 1e-06
F32 = jnp.float32
BF16 = jnp.bfloat16
MESH = pl.DeviceIdType.MESH


def sigmoid(v):
    return 0.5 * jnp.tanh(0.5 * v) + 0.5


def silu_grad(pre, sig):
    return sig * (1.0 + pre * (1.0 - sig))


def lpips_grad(first, second, linear):
    chans = first.shape[-1]
    inv_first = lax.rsqrt(jnp.sum(first * first, -1, keepdims=True) + chans * EPS)
    inv_second = lax.rsqrt(jnp.sum(second * second, -1, keepdims=True) + chans * EPS)
    unit = first * inv_first
    weighted = linear * (unit - second * inv_second)
    along = jnp.sum(weighted * unit, -1, keepdims=True)
    return (weighted - unit * along) * (2.0 * inv_first)


def expand(ref, lead, chans):
    centre = ref[lead + (slice(None), pl.ds(chans, chans))]
    width = centre.shape[0]
    wide = centre.astype(F32)
    col = lax.broadcasted_iota(jnp.int32, wide.shape, 0)
    before = jnp.where(col == 0, 0.0, pltpu.roll(wide, 1, 0)).astype(BF16)
    after = jnp.where(col == width - 1, 0.0, pltpu.roll(wide, width - 1, 0)).astype(BF16)
    ref[lead + (slice(None), pl.ds(0, chans))] = before
    ref[lead + (slice(None), pl.ds(2 * chans, chans))] = after


def dot_nt(a, b):
    return lax.dot_general(a, b, (((1,), (1,)), ((), ())), preferred_element_type=F32)


def kernel(
    n, img, w3h, w4h, b3, b4, l3, l4, out,
    x3, w3, w4, p3, g4, g3, gate, near, fold, grow, outv,
    local_sem, out_sem, send_sem, recv_sem,
):
    rows = img.shape[1]
    half = rows // 2
    c3 = w3.shape[3]
    c4 = w4.shape[3]
    width = img.shape[2]
    mid = width // 2
    group = lax.axis_index("groups")
    pos = lax.axis_index("rows")
    has_up = pos > 0
    has_down = pos < n - 1

    in_copies = [
        pltpu.make_async_copy(img, x3.at[:, pl.ds(1, rows), :, pl.ds(c3, c3)], local_sem.at[0]),
        pltpu.make_async_copy(w3h, w3, local_sem.at[1]),
        pltpu.make_async_copy(w4h, w4, local_sem.at[2]),
    ]
    for copy in in_copies:
        copy.start()

    barrier = pltpu.get_barrier_semaphore()

    @pl.when(has_up)
    def _():
        pl.semaphore_signal(barrier, inc=1, device_id=(group, pos - 1), device_id_type=MESH)

    @pl.when(has_down)
    def _():
        pl.semaphore_signal(barrier, inc=1, device_id=(group, pos + 1), device_id_type=MESH)

    pl.semaphore_wait(barrier, has_up.astype(jnp.int32) + has_down.astype(jnp.int32))

    def halo(which, src_last, dst_first, src_first, dst_last):
        down = pltpu.make_async_remote_copy(
            src_ref=src_last, dst_ref=dst_first,
            send_sem=send_sem.at[which, 0], recv_sem=recv_sem.at[which, 0],
            device_id=(group, pos + 1), device_id_type=MESH,
        )
        up = pltpu.make_async_remote_copy(
            src_ref=src_first, dst_ref=dst_last,
            send_sem=send_sem.at[which, 1], recv_sem=recv_sem.at[which, 1],
            device_id=(group, pos - 1), device_id_type=MESH,
        )

        def start():
            @pl.when(has_down)
            def _():
                down.start()

            @pl.when(has_up)
            def _():
                up.start()

        def arrive():
            @pl.when(has_up)
            def _():
                down.wait_recv()

            @pl.when(jnp.logical_not(has_up))
            def _():
                dst_first[...] = jnp.zeros(dst_first.shape, BF16)

            @pl.when(has_down)
            def _():
                up.wait_recv()

            @pl.when(jnp.logical_not(has_down))
            def _():
                dst_last[...] = jnp.zeros(dst_last.shape, BF16)

        def sent():
            @pl.when(has_down)
            def _():
                down.wait_send()

            @pl.when(has_up)
            def _():
                up.wait_send()

        return start, arrive, sent

    at3 = lambda row: x3.at[:, row, :, pl.ds(c3, c3)]
    atp = lambda row: p3.at[:, row, :, pl.ds(c3, c3)]
    at4 = lambda row: g4.at[row, :, pl.ds(c4, c4)]
    atg = lambda row: g3.at[row, :, pl.ds(c3, c3)]
    halos = [
        halo(0, img.at[:, rows - 1], at3(0), img.at[:, 0], at3(rows + 1)),
        halo(1, atp(half), atp(0), atp(1), atp(half + 1)),
        halo(2, at4(half), at4(0), at4(1), at4(half + 1)),
        halo(3, atg(rows), atg(0), atg(1), atg(rows + 1)),
    ]
    halos[0][0]()
    in_copies[0].wait()

    @pl.loop(1, rows + 1)
    def _(row):
        for m in range(2):
            expand(x3, (m, row), c3)

    in_copies[1].wait()

    def third(pair):
        bias = b3[...]
        linear = l3[...]
        kern = w3[...].reshape(9 * c3, c3)
        acts = []
        for j in range(2):
            row = 2 * pair + j
            pres = []
            for m in range(2):
                lhs = jnp.concatenate([x3[m, row + a] for a in range(3)], axis=1)
                pres.append(jnp.dot(lhs, kern, preferred_element_type=F32) + bias)
            sigs = [sigmoid(v) for v in pres]
            act = [(v * s).astype(BF16).astype(F32) for v, s in zip(pres, sigs)]
            slope = silu_grad(pres[0], sigs[0])
            gate[row] = slope
            near[row] = lpips_grad(act[0], act[1], linear) * slope
            acts.append(act)
        for m in range(2):
            total = acts[0][m] + acts[1][m]
            for k in range(c3 // 128):
                fold[m, k] = total[:, k * 128 : (k + 1) * 128]
            for k in range(c3 // 128):
                even = fold[m, k, pl.ds(0, mid, 2), :]
                odd = fold[m, k, pl.ds(1, mid, 2), :]
                p3[m, pair + 1, :, pl.ds(c3 + k * 128, 128)] = (0.25 * (even + odd)).astype(BF16)
            expand(p3, (m, pair + 1), c3)

    pl.loop(1, half - 1)(third)
    halos[0][1]()
    for m in range(2):
        expand(x3, (m, 0), c3)
        expand(x3, (m, rows + 1), c3)
    pl.loop(0, 2)(lambda i: third(i * (half - 1)))
    halos[1][0]()

    in_copies[2].wait()

    def fourth(one, two):
        kern = w4[...].reshape(9 * c3, c4)
        pres = []
        for m in range(2):
            lhs = jnp.concatenate(
                [
                    jnp.concatenate([p3[m, row + a] for a in range(3)], axis=1)
                    for row in (one, two)
                ],
                axis=0,
            )
            pres.append(jnp.dot(lhs, kern, preferred_element_type=F32) + b4[...])
        sigs = [sigmoid(v) for v in pres]
        slope = silu_grad(pres[0], sigs[0])
        grad = lpips_grad(pres[0] * sigs[0], pres[1] * sigs[1], l4[...]) * slope
        grad = grad.astype(BF16)
        for k, row in enumerate((one, two)):
            g4[row + 1, :, pl.ds(c4, c4)] = grad[k * mid : (k + 1) * mid]

    pairs = [(row, row + 1) for row in range(1, half - 1, 2)]
    for one, two in pairs:
        fourth(one, two)
    halos[1][1]()
    for m in range(2):
        expand(p3, (m, 0), c3)
        expand(p3, (m, half + 1), c3)
    fourth(0, half - 1)
    halos[2][0]()

    @pl.loop(1, half + 1)
    def _(row):
        expand(g4, (row,), c4)

    def third_grad(one, two):
        total = None
        for a in range(3):
            for b in range(3):
                part = pl.ds((2 - b) * c4, c4)
                lhs = jnp.concatenate([g4[row + 2 - a, :, part] for row in (one, two)], axis=0)
                term = dot_nt(lhs, w4[a, b])
                total = term if total is None else total + term
        total = 0.25 * total
        for k, row in enumerate((one, two)):
            for h in range(c3 // 128):
                piece = total[k * mid : (k + 1) * mid, h * 128 : (h + 1) * 128]
                grow[k, h, pl.ds(0, mid, 2), :] = piece
                grow[k, h, pl.ds(1, mid, 2), :] = piece
            for j in range(2):
                for h in range(c3 // 128):
                    lanes = pl.ds(h * 128, 128)
                    value = grow[k, h] * gate[2 * row + j, :, lanes] + near[2 * row + j, :, lanes]
                    g3[2 * row + j + 1, :, pl.ds(c3 + h * 128, 128)] = value.astype(BF16)

    for one, two in pairs:
        third_grad(one, two)
    halos[2][1]()
    expand(g4, (0,), c4)
    expand(g4, (half + 1,), c4)
    third_grad(0, half - 1)
    halos[3][0]()

    @pl.loop(1, rows + 1)
    def _(row):
        expand(g3, (row,), c3)

    def result(one, two):
        total = None
        for a in range(3):
            for b in range(3):
                part = pl.ds((2 - b) * c3, c3)
                lhs = jnp.concatenate([g3[row + 2 - a, :, part] for row in (one, two)], axis=0)
                term = dot_nt(lhs, w3[a, b])
                total = term if total is None else total + term
        outv[one] = total[:width]
        outv[two] = total[width:]

    pl.loop(0, half - 1)(lambda i: result(2 * i + 1, 2 * i + 2))
    inner = pltpu.make_async_copy(
        outv.at[pl.ds(1, rows - 2)], out.at[pl.ds(1, rows - 2)], out_sem.at[0]
    )
    inner.start()
    halos[3][1]()
    expand(g3, (0,), c3)
    expand(g3, (rows + 1,), c3)
    result(0, rows - 1)
    first = pltpu.make_async_copy(outv.at[0], out.at[0], out_sem.at[1])
    last = pltpu.make_async_copy(outv.at[rows - 1], out.at[rows - 1], out_sem.at[2])
    first.start()
    last.start()
    for each in halos:
        each[2]()
    inner.wait()
    first.wait()
    last.wait()


def local(
    images, third_weight, third_bias, fourth_weight, fourth_bias, third_linear, fourth_linear
):
    n = lax.axis_size("rows")
    _, rows, width, c3 = images.shape
    c4 = fourth_weight.shape[3]
    half, mid = rows // 2, width // 2
    anywhere = pl.BlockSpec(memory_space=pl.ANY)
    vmem = pl.BlockSpec(memory_space=pltpu.VMEM)
    return pl.pallas_call(
        functools.partial(kernel, n),
        out_shape=jax.ShapeDtypeStruct((rows, width, c3), F32),
        in_specs=[anywhere] * 3 + [vmem] * 4,
        out_specs=anywhere,
        scratch_shapes=[
            pltpu.VMEM((2, rows + 2, width, 3 * c3), BF16),
            pltpu.VMEM(third_weight.shape, BF16),
            pltpu.VMEM(fourth_weight.shape, BF16),
            pltpu.VMEM((2, half + 2, mid, 3 * c3), BF16),
            pltpu.VMEM((half + 2, mid, 3 * c4), BF16),
            pltpu.VMEM((rows + 2, width, 3 * c3), BF16),
            pltpu.VMEM((rows, width, c3), F32),
            pltpu.VMEM((rows, width, c3), F32),
            pltpu.VMEM((2, c3 // 128, width, 128), F32),
            pltpu.VMEM((2, c3 // 128, width, 128), F32),
            pltpu.VMEM((rows, width, c3), F32),
            pltpu.SemaphoreType.DMA((3,)),
            pltpu.SemaphoreType.DMA((3,)),
            pltpu.SemaphoreType.DMA((4, 2)),
            pltpu.SemaphoreType.DMA((4, 2)),
        ],
        compiler_params=pltpu.CompilerParams(
            collective_id=0, has_side_effects=True, vmem_limit_bytes=56 * 2**20
        ),
    )(
        images, third_weight, fourth_weight,
        third_bias.reshape(1, c3), fourth_bias.reshape(1, c4),
        third_linear.reshape(1, c3), fourth_linear.reshape(1, c4),
    )


def solution(mesh):
    return jax.shard_map(
        local,
        mesh=mesh,
        in_specs=(P(None, ("groups", "rows"), None, None), P(), P(), P(), P(), P(), P()),
        out_specs=P(("groups", "rows"), None, None),
        check_vma=False,
    )
```

time: 120 us -> 34.8 us (0.29)
  other arithmetic: 39 us -> 0 us
  Pallas kernels: 0 us -> 31.6 us
  local copies, waits for them, and re-layouts: 29.1 us -> 3.05 us
  starting transfers between devices: 20.9 us -> 0 us
  matrix products: 16.9 us -> 0 us
  waiting for transfers between devices: 13.3 us -> 0 us
    pallas_call x0 -> x1, Pallas kernels: none -> 31.6 us  [local(): pl.pallas_call(functools.partial(kernel, n), out_shape=jax.ShapeDtypeStru...]
    ppermute x8 -> x0, starting transfers between devices: 20.9 us -> none  [the longest x4 12 us: padded_2(): lax.ppermute(lax.slice_in_dim(block, block.shape[dim] - width, None, axis...]
    mul x3 -> x0, other arithmetic: 19.9 us -> none  [the longest x2 19.3 us: lpips_grad(): unit_first * jnp.sum(weighted * unit_first, -1, keepdims=True)]
    dot_general x12 -> x0, matrix products: 16.9 us -> none  [the longest x6 10.7 us: conv_rows(): jnp.dot(joined.reshape(-1, 3 * chans), weight[offset].reshape(3 * chans,...]
    ppermute x8 -> x0, waiting for transfers between devices: 13.3 us -> none  [the longest x4 13.3 us: padded_2(): lax.ppermute(lax.slice_in_dim(block, 0, width, axis=dim), axis, backward)]
    concatenate x8 -> x0, other arithmetic: 11 us -> none  [the longest x2 6.78 us: conv_rows(): jnp.concatenate([strip[:, :, 0:width], strip[:, :, 1:width + 1], strip[:,...]
    transpose x8 -> x0, local copies, waits for them, and re-layouts: 10.8 us -> none  [conv_back(): flipped = jnp.transpose(weight[offset], (0, 2, 1)).reshape(3 * outputs, -1)]
    slice x8 -> x0, local copies, waits for them, and re-layouts: 7.98 us -> none  [the longest x2 4.79 us: conv_rows(): strip[:, :, 0:width]]
  transfers between devices with their start and end apart: 8 -> 0, of which waited for: 3 -> 0; matrix products, arithmetic and copies ran while one was open for 10% -> 0% of each run, Pallas kernels for 0% -> 0%
where the time goes in v1:
time: 34.8 us; the launch traced here: 34.6 us
  Pallas kernels  31.6 us (91%)
  local copies, waits for them, and re-layouts  3.05 us (9%)
    pallas_call x1, Pallas kernels, local(): pl.pallas_call(functools.partial(kernel, n), out_shape=jax.ShapeDtypeStru...  31.6 us
    unnamed x1, local copies, waits for them, and re-layouts  3.05 us

profile of v1, /device:TPU:1, one launch (start us, length us, event | category | flops | bytes accessed | tf_op | source)
XLA Modules:
  0.0 34.6 jit_solution(2243563932360974454)
XLA Ops:
  0.0 31.6 %shard_map.73 = f32[8,256,256]{2,1,0:T(8,128)} custom-call(bf16[2,8,256,256]{3,2,1,0:T(8,128)(2,1)} %img.1, bf16[3,3,256,256]{3,2,1,0:T(8,128)(2,1)} %w3h.1, bf16[3,3,256,512]{3,2,1,0:T(8,128)(2,1)} %w4h.1, f32[1,256]{1,0:T(1,128)} %bitcast.6, f32[1,512]{1,0:T(1,128)} %bitcast.4, f32[1,256]{1,0:T(1,128)} %bitcast.7, f32[1,512]{1,0:T(1,128)} %bitcast.5), custom_call_target="tpu_custom_call" | custom-call | tf_op jit(solution)/shard_map/pallas_call | solution.py:295
  31.6 3.0 %copy.9 = f32[8,256,256]{2,1,0:T(8,128)} copy(f32[8,256,256]{2,1,0:T(8,128)} %shard_map.73) | data formatting | bytes 4194304

commit v2 on v1

--- a/solution.py
+++ b/solution.py
@@ -47,7 +47,7 @@
 
 def kernel(
     n, img, w3h, w4h, b3, b4, l3, l4, out,
-    x3, w3, w4, p3, g4, g3, gate, near, fold, grow, outv,
+    x3, w3, w4, p3, g4, g3, gate, near, fold, grow, outv, part3, acts3, part4, partb,
     local_sem, out_sem, send_sem, recv_sem,
 ):
     rows = img.shape[1]
@@ -149,6 +149,53 @@
             expand(x3, (m, row), c3)
 
     in_copies[1].wait()
+
+    def pool(m, pair, total):
+        for k in range(c3 // 128):
+            fold[m, k] = total[:, k * 128 : (k + 1) * 128]
+        for k in range(c3 // 128):
+            even = fold[m, k, pl.ds(0, mid, 2), :]
+            odd = fold[m, k, pl.ds(1, mid, 2), :]
+            p3[m, pair + 1, :, pl.ds(c3 + k * 128, 128)] = (0.25 * (even + odd)).astype(BF16)
+
+    edges = [(0, 0, 1, (1, 2), 0), (1, rows - 1, rows - 2, (0, 1), 2)]
+
+    def third_early(edge, row, partner, taps, _):
+        kern = w3[...].reshape(9 * c3, c3)
+        some = w3[pl.ds(taps[0], 2)].reshape(6 * c3, c3)
+        pres = []
+        for m in range(2):
+            lhs = jnp.concatenate([x3[m, partner + a] for a in range(3)], axis=1)
+            pres.append(jnp.dot(lhs, kern, preferred_element_type=F32) + b3[...])
+            lhs = jnp.concatenate([x3[m, row + a] for a in taps], axis=1)
+            part3[edge, m] = jnp.dot(lhs, some, preferred_element_type=F32) + b3[...]
+        sigs = [sigmoid(v) for v in pres]
+        act = [(v * s).astype(BF16).astype(F32) for v, s in zip(pres, sigs)]
+        slope = silu_grad(pres[0], sigs[0])
+        gate[partner] = slope
+        near[partner] = lpips_grad(act[0], act[1], l3[...]) * slope
+        for m in range(2):
+            acts3[edge, m] = act[m]
+
+    def third_late(edge, row, partner, taps, tap):
+        kern = w3[tap].reshape(3 * c3, c3)
+        for m in range(2):
+            pre = part3[edge, m] + jnp.dot(
+                x3[m, row + tap], kern, preferred_element_type=F32
+            )
+            act = (pre * sigmoid(pre)).astype(BF16).astype(F32)
+            pool(m, row // 2, act + acts3[edge, m])
+            acts3[edge, m] = act
+            if m == 0:
+                part3[edge, m] = pre
+
+    def third_near(edge, row, partner, taps, tap):
+        pre = part3[edge, 0]
+        slope = silu_grad(pre, sigmoid(pre))
+        gate[row] = slope
+        near[row] = lpips_grad(acts3[edge, 0], acts3[edge, 1], l3[...]) * slope
+        for m in range(2):
+            expand(p3, (m, row // 2 + 1), c3)
 
     def third(pair):
         bias = b3[...]
@@ -169,21 +216,21 @@
             acts.append(act)
         for m in range(2):
             total = acts[0][m] + acts[1][m]
-            for k in range(c3 // 128):
-                fold[m, k] = total[:, k * 128 : (k + 1) * 128]
-            for k in range(c3 // 128):
-                even = fold[m, k, pl.ds(0, mid, 2), :]
-                odd = fold[m, k, pl.ds(1, mid, 2), :]
-                p3[m, pair + 1, :, pl.ds(c3 + k * 128, 128)] = (0.25 * (even + odd)).astype(BF16)
+            pool(m, pair, total)
             expand(p3, (m, pair + 1), c3)
 
     pl.loop(1, half - 1)(third)
+    for edge in edges:
+        third_early(*edge)
     halos[0][1]()
     for m in range(2):
         expand(x3, (m, 0), c3)
         expand(x3, (m, rows + 1), c3)
-    pl.loop(0, 2)(lambda i: third(i * (half - 1)))
+    for edge in edges:
+        third_late(*edge)
     halos[1][0]()
+    for edge in edges:
+        third_near(*edge)
 
     in_copies[2].wait()
 
@@ -199,6 +246,9 @@
                 axis=0,
             )
             pres.append(jnp.dot(lhs, kern, preferred_element_type=F32) + b4[...])
+        fourth_grad(pres, one, two)
+
+    def fourth_grad(pres, one, two):
         sigs = [sigmoid(v) for v in pres]
         slope = silu_grad(pres[0], sigs[0])
         grad = lpips_grad(pres[0] * sigs[0], pres[1] * sigs[1], l4[...]) * slope
@@ -206,14 +256,37 @@
         for k, row in enumerate((one, two)):
             g4[row + 1, :, pl.ds(c4, c4)] = grad[k * mid : (k + 1) * mid]
 
+    coarse = [(0, 0, (1, 2), 0), (1, half - 1, (0, 1), 2)]
+
+    def fourth_early(edge, row, taps, _):
+        kern = w4[pl.ds(taps[0], 2)].reshape(6 * c3, c4)
+        lhs = jnp.concatenate(
+            [jnp.concatenate([p3[m, row + a] for a in taps], axis=1) for m in range(2)], axis=0
+        )
+        part4[edge] = jnp.dot(lhs, kern, preferred_element_type=F32) + b4[...]
+
+    def fourth_late():
+        whole = []
+        for edge, row, _, tap in coarse:
+            lhs = jnp.concatenate([p3[m, row + tap] for m in range(2)], axis=0)
+            kern = w4[tap].reshape(3 * c3, c4)
+            whole.append(part4[edge] + jnp.dot(lhs, kern, preferred_element_type=F32))
+        pres = [
+            jnp.concatenate([v[m * mid : (m + 1) * mid] for v in whole], axis=0)
+            for m in range(2)
+        ]
+        fourth_grad(pres, 0, half - 1)
+
     pairs = [(row, row + 1) for row in range(1, half - 1, 2)]
     for one, two in pairs:
         fourth(one, two)
+    for edge in coarse:
+        fourth_early(*edge)
     halos[1][1]()
     for m in range(2):
         expand(p3, (m, 0), c3)
         expand(p3, (m, half + 1), c3)
-    fourth(0, half - 1)
+    fourth_late()
     halos[2][0]()
 
     @pl.loop(1, half + 1)
@@ -228,7 +301,9 @@
                 lhs = jnp.concatenate([g4[row + 2 - a, :, part] for row in (one, two)], axis=0)
                 term = dot_nt(lhs, w4[a, b])
                 total = term if total is None else total + term
-        total = 0.25 * total
+        third_value(0.25 * total, one, two)
+
+    def third_value(total, one, two):
         for k, row in enumerate((one, two)):
             for h in range(c3 // 128):
                 piece = total[k * mid : (k + 1) * mid, h * 128 : (h + 1) * 128]
@@ -242,10 +317,26 @@
 
     for one, two in pairs:
         third_grad(one, two)
+
+    def back(ref, kern, chans, row, taps):
+        total = None
+        for a in taps:
+            for b in range(3):
+                lhs = ref[row + 2 - a, :, pl.ds((2 - b) * chans, chans)]
+                term = dot_nt(lhs, kern[a, b])
+                total = term if total is None else total + term
+        return total
+
+    partb[0] = back(g4, w4, c4, 0, (0, 1))
+    partb[1] = back(g4, w4, c4, half - 1, (1, 2))
     halos[2][1]()
     expand(g4, (0,), c4)
     expand(g4, (half + 1,), c4)
-    third_grad(0, half - 1)
+    ends = [
+        partb[0] + back(g4, w4, c4, 0, (2,)),
+        partb[1] + back(g4, w4, c4, half - 1, (0,)),
+    ]
+    third_value(0.25 * jnp.concatenate(ends, axis=0), 0, half - 1)
     halos[3][0]()
 
     @pl.loop(1, rows + 1)
@@ -268,10 +359,13 @@
         outv.at[pl.ds(1, rows - 2)], out.at[pl.ds(1, rows - 2)], out_sem.at[0]
     )
     inner.start()
+    outv[0] = back(g3, w3, c3, 0, (0, 1))
+    outv[rows - 1] = back(g3, w3, c3, rows - 1, (1, 2))
     halos[3][1]()
     expand(g3, (0,), c3)
     expand(g3, (rows + 1,), c3)
-    result(0, rows - 1)
+    outv[0] = outv[0] + back(g3, w3, c3, 0, (2,))
+    outv[rows - 1] = outv[rows - 1] + back(g3, w3, c3, rows - 1, (0,))
     first = pltpu.make_async_copy(outv.at[0], out.at[0], out_sem.at[1])
     last = pltpu.make_async_copy(outv.at[rows - 1], out.at[rows - 1], out_sem.at[2])
     first.start()
@@ -309,6 +403,10 @@
             pltpu.VMEM((2, c3 // 128, width, 128), F32),
             pltpu.VMEM((2, c3 // 128, width, 128), F32),
             pltpu.VMEM((rows, width, c3), F32),
+            pltpu.VMEM((2, 2, width, c3), F32),
+            pltpu.VMEM((2, 2, width, c3), F32),
+            pltpu.VMEM((2, 2 * mid, c4), F32),
+            pltpu.VMEM((2, mid, c3), F32),
             pltpu.SemaphoreType.DMA((3,)),
             pltpu.SemaphoreType.DMA((3,)),
             pltpu.SemaphoreType.DMA((4, 2)),

time: 34.8 us -> 31.1 us (0.89)
  Pallas kernels: 31.6 us -> 27.8 us
    pallas_call x1, Pallas kernels: 31.6 us -> 27.8 us  [local(): pl.pallas_call(functools.partial(kernel, n), out_shape=jax.ShapeDtypeStru...]
where the time goes in v2:
time: 31.1 us; the launch traced here: 30.9 us
  Pallas kernels  27.8 us (89%)
  local copies, waits for them, and re-layouts  3.05 us (10%)
    pallas_call x1, Pallas kernels, local(): pl.pallas_call(functools.partial(kernel, n), out_shape=jax.ShapeDtypeStru...  27.8 us
    unnamed x1, local copies, waits for them, and re-layouts  3.05 us

profile of v2, /device:TPU:1, one launch (start us, length us, event | category | flops | bytes accessed | tf_op | source)
XLA Modules:
  0.0 30.9 jit_solution(17966336033725999785)
XLA Ops:
  0.0 27.8 %shard_map.73 = f32[8,256,256]{2,1,0:T(8,128)} custom-call(bf16[2,8,256,256]{3,2,1,0:T(8,128)(2,1)} %img.1, bf16[3,3,256,256]{3,2,1,0:T(8,128)(2,1)} %w3h.1, bf16[3,3,256,512]{3,2,1,0:T(8,128)(2,1)} %w4h.1, f32[1,256]{1,0:T(1,128)} %bitcast.6, f32[1,512]{1,0:T(1,128)} %bitcast.4, f32[1,256]{1,0:T(1,128)} %bitcast.7, f32[1,512]{1,0:T(1,128)} %bitcast.5), custom_call_target="tpu_custom_call" | custom-call | tf_op jit(solution)/shard_map/pallas_call | solution.py:389
  27.8 3.0 %copy.9 = f32[8,256,256]{2,1,0:T(8,128)} copy(f32[8,256,256]{2,1,0:T(8,128)} %shard_map.73) | data formatting | bytes 4194304

commit v3 on v2

--- a/solution.py
+++ b/solution.py
@@ -93,29 +93,29 @@
             device_id=(group, pos - 1), device_id_type=MESH,
         )
 
-        def start():
-            @pl.when(has_down)
+        def start(edge):
+            @pl.when((edge == 1) & has_down)
             def _():
                 down.start()
 
-            @pl.when(has_up)
+            @pl.when((edge == 0) & has_up)
             def _():
                 up.start()
 
-        def arrive():
-            @pl.when(has_up)
+        def arrive(edge):
+            @pl.when((edge == 0) & has_up)
             def _():
                 down.wait_recv()
 
-            @pl.when(jnp.logical_not(has_up))
+            @pl.when((edge == 0) & jnp.logical_not(has_up))
             def _():
                 dst_first[...] = jnp.zeros(dst_first.shape, BF16)
 
-            @pl.when(has_down)
+            @pl.when((edge == 1) & has_down)
             def _():
                 up.wait_recv()
 
-            @pl.when(jnp.logical_not(has_down))
+            @pl.when((edge == 1) & jnp.logical_not(has_down))
             def _():
                 dst_last[...] = jnp.zeros(dst_last.shape, BF16)
 
@@ -140,7 +140,16 @@
         halo(2, at4(half), at4(0), at4(1), at4(half + 1)),
         halo(3, atg(rows), atg(0), atg(1), atg(rows + 1)),
     ]
-    halos[0][0]()
+    halos[0][0](0)
+    halos[0][0](1)
+
+    def sides(which, body):
+        @pl.loop(0, 2)
+        def _(i):
+            edge = lax.rem(i + 1 + lax.rem(pos, 2), 2)
+            halos[which][1](edge)
+            body(edge)
+
     in_copies[0].wait()
 
     @pl.loop(1, rows + 1)
@@ -177,17 +186,16 @@
         for m in range(2):
             acts3[edge, m] = act[m]
 
-    def third_late(edge, row, partner, taps, tap):
+    def third_late(edge, row, pair, tap):
         kern = w3[tap].reshape(3 * c3, c3)
         for m in range(2):
             pre = part3[edge, m] + jnp.dot(
                 x3[m, row + tap], kern, preferred_element_type=F32
             )
             act = (pre * sigmoid(pre)).astype(BF16).astype(F32)
-            pool(m, row // 2, act + acts3[edge, m])
+            pool(m, pair, act + acts3[edge, m])
             acts3[edge, m] = act
-            if m == 0:
-                part3[edge, m] = pre
+            part3[edge, m] = pre
 
     def third_near(edge, row, partner, taps, tap):
         pre = part3[edge, 0]
@@ -222,13 +230,14 @@
     pl.loop(1, half - 1)(third)
     for edge in edges:
         third_early(*edge)
-    halos[0][1]()
-    for m in range(2):
-        expand(x3, (m, 0), c3)
-        expand(x3, (m, rows + 1), c3)
-    for edge in edges:
-        third_late(*edge)
-    halos[1][0]()
+
+    def third_side(edge):
+        for m in range(2):
+            expand(x3, (m, edge * (rows + 1)), c3)
+        third_late(edge, edge * (rows - 1), edge * (half - 1), 2 * edge)
+        halos[1][0](edge)
+
+    sides(0, third_side)
     for edge in edges:
         third_near(*edge)
 
@@ -282,12 +291,14 @@
         fourth(one, two)
     for edge in coarse:
         fourth_early(*edge)
-    halos[1][1]()
+    halos[1][1](0)
+    halos[1][1](1)
     for m in range(2):
         expand(p3, (m, 0), c3)
         expand(p3, (m, half + 1), c3)
     fourth_late()
-    halos[2][0]()
+    halos[2][0](0)
+    halos[2][0](1)
 
     @pl.loop(1, half + 1)
     def _(row):
@@ -303,8 +314,8 @@
                 total = term if total is None else total + term
         third_value(0.25 * total, one, two)
 
-    def third_value(total, one, two):
-        for k, row in enumerate((one, two)):
+    def third_value(total, *places):
+        for k, row in enumerate(places):
             for h in range(c3 // 128):
                 piece = total[k * mid : (k + 1) * mid, h * 128 : (h + 1) * 128]
                 grow[k, h, pl.ds(0, mid, 2), :] = piece
@@ -329,15 +340,15 @@
 
     partb[0] = back(g4, w4, c4, 0, (0, 1))
     partb[1] = back(g4, w4, c4, half - 1, (1, 2))
-    halos[2][1]()
-    expand(g4, (0,), c4)
-    expand(g4, (half + 1,), c4)
-    ends = [
-        partb[0] + back(g4, w4, c4, 0, (2,)),
-        partb[1] + back(g4, w4, c4, half - 1, (0,)),
-    ]
-    third_value(0.25 * jnp.concatenate(ends, axis=0), 0, half - 1)
-    halos[3][0]()
+
+    def back_side(edge):
+        row = edge * (half - 1)
+        expand(g4, (edge * (half + 1),), c4)
+        total = partb[edge] + back(g4, w4, c4, row, (2 - 2 * edge,))
+        third_value(0.25 * total, row)
+        halos[3][0](edge)
+
+    sides(2, back_side)
 
     @pl.loop(1, rows + 1)
     def _(row):
@@ -351,21 +362,24 @@
                 lhs = jnp.concatenate([g3[row + 2 - a, :, part] for row in (one, two)], axis=0)
                 term = dot_nt(lhs, w3[a, b])
                 total = term if total is None else total + term
-        outv[one] = total[:width]
-        outv[two] = total[width:]
+        outv[one] = total[:width].astype(BF16)
+        outv[two] = total[width:].astype(BF16)
 
     pl.loop(0, half - 1)(lambda i: result(2 * i + 1, 2 * i + 2))
     inner = pltpu.make_async_copy(
         outv.at[pl.ds(1, rows - 2)], out.at[pl.ds(1, rows - 2)], out_sem.at[0]
     )
     inner.start()
-    outv[0] = back(g3, w3, c3, 0, (0, 1))
-    outv[rows - 1] = back(g3, w3, c3, rows - 1, (1, 2))
-    halos[3][1]()
-    expand(g3, (0,), c3)
-    expand(g3, (rows + 1,), c3)
-    outv[0] = outv[0] + back(g3, w3, c3, 0, (2,))
-    outv[rows - 1] = outv[rows - 1] + back(g3, w3, c3, rows - 1, (0,))
+    part3[0, 0] = back(g3, w3, c3, 0, (0, 1))
+    part3[1, 0] = back(g3, w3, c3, rows - 1, (1, 2))
+
+    def last_side(edge):
+        row = edge * (rows - 1)
+        expand(g3, (edge * (rows + 1),), c3)
+        total = part3[edge, 0] + back(g3, w3, c3, row, (2 - 2 * edge,))
+        outv[row] = total.astype(BF16)
+
+    sides(3, last_side)
     first = pltpu.make_async_copy(outv.at[0], out.at[0], out_sem.at[1])
     last = pltpu.make_async_copy(outv.at[rows - 1], out.at[rows - 1], out_sem.at[2])
     first.start()
@@ -388,7 +402,7 @@
     vmem = pl.BlockSpec(memory_space=pltpu.VMEM)
     return pl.pallas_call(
         functools.partial(kernel, n),
-        out_shape=jax.ShapeDtypeStruct((rows, width, c3), F32),
+        out_shape=jax.ShapeDtypeStruct((rows, width, c3), BF16),
         in_specs=[anywhere] * 3 + [vmem] * 4,
         out_specs=anywhere,
         scratch_shapes=[
@@ -402,7 +416,7 @@
             pltpu.VMEM((rows, width, c3), F32),
             pltpu.VMEM((2, c3 // 128, width, 128), F32),
             pltpu.VMEM((2, c3 // 128, width, 128), F32),
-            pltpu.VMEM((rows, width, c3), F32),
+            pltpu.VMEM((rows, width, c3), BF16),
             pltpu.VMEM((2, 2, width, c3), F32),
             pltpu.VMEM((2, 2, width, c3), F32),
             pltpu.VMEM((2, 2 * mid, c4), F32),
@@ -419,7 +433,7 @@
         images, third_weight, fourth_weight,
         third_bias.reshape(1, c3), fourth_bias.reshape(1, c4),
         third_linear.reshape(1, c3), fourth_linear.reshape(1, c4),
-    )
+    ).astype(F32)
 
 
 def solution(mesh):

time: 31.1 us -> 30.3 us (0.974)
  local copies, waits for them, and re-layouts: 3.05 us -> 0 us
  other arithmetic: 0 us -> 2.73 us
  Pallas kernels: 27.8 us -> 27.4 us
    unnamed x1 -> x0, local copies, waits for them, and re-layouts: 3.05 us -> none
    convert_element_type x0 -> x1, other arithmetic: none -> 2.73 us  [local(): return pl.pallas_call(functools.partial(kernel, n), out_shape=jax.ShapeDt...]
    pallas_call x1, Pallas kernels: 27.8 us -> 27.4 us  [local(): pl.pallas_call(functools.partial(kernel, n), out_shape=jax.ShapeDtypeStru...]
where the time goes in v3:
time: 30.3 us; the launch traced here: 30.2 us
  Pallas kernels  27.4 us (90%)
  other arithmetic  2.73 us (9%)
    pallas_call x1, Pallas kernels, local(): pl.pallas_call(functools.partial(kernel, n), out_shape=jax.ShapeDtypeStru...  27.4 us
    convert_element_type x1, other arithmetic, local(): return pl.pallas_call(functools.partial(kernel, n), out_shape=jax.ShapeDt...  2.73 us

profile of v3, /device:TPU:1, one launch (start us, length us, event | category | flops | bytes accessed | tf_op | source)
XLA Modules:
  0.0 30.2 jit_solution(17429432685075773530)
XLA Ops:
  0.0 27.4 %shard_map.73 = bf16[8,256,256]{2,1,0:T(8,128)(2,1)} custom-call(bf16[2,8,256,256]{3,2,1,0:T(8,128)(2,1)} %img.1, bf16[3,3,256,256]{3,2,1,0:T(8,128)(2,1)} %w3h.1, bf16[3,3,256,512]{3,2,1,0:T(8,128)(2,1)} %w4h.1, f32[1,256]{1,0:T(1,128)} %bitcast.6, f32[1,512]{1,0:T(1,128)} %bitcast.4, f32[1,256]{1,0:T(1,128)} %bitcast.7, f32[1,512]{1,0:T(1,128)} %bitcast.5), custom_call_target="tpu_custom_call" | custom-call | tf_op jit(solution)/shard_map/pallas_call | solution.py:403
  27.4 2.7 %convert_element_type.3 = f32[8,256,256]{2,1,0:T(8,128)} convert(bf16[8,256,256]{2,1,0:T(8,128)(2,1)} %shard_map.73) | non-fusion elementwise | flops 524288 | bytes 3145728 | tf_op jit(solution)/shard_map/convert_element_type | solution.py:436
